TPU v7x, 256 devices: a whole 4x4x8 slice. The times are simulated.
256 devices in a mesh: pipe: 16 (over y, z_lo), fsdp: 16 (over z_hi, x, core).
Axes of the slice: x: 4, y: 4, z: 8 (z_hi: 2, z_lo: 4; z = z_hi * 4 + z_lo), core: 2. Of those that a mesh axis runs over, the one named last changes fastest.
Arguments:
- latents: bfloat16 [4, 512, 6144], P(None, 'fsdp'), may hold values from -6 to 6
- upstream: bfloat16 [4, 512, 6144], P(None, 'fsdp'), may hold values from -0.1875 to 0.1875
- proj_in: bfloat16 [16, 6144, 256], P('pipe', 'fsdp'), may hold values from -0.078125 to 0.078125
- proj_out: bfloat16 [16, 256, 6144], P('pipe', None, 'fsdp'), may hold values from -0.375 to 0.375
- norm_gain: float32 [16, 6144], P('pipe'), may hold values from 0.1 to 1.9
Outputs:
- grad_in: bfloat16 [16, 6144, 256], P('pipe', 'fsdp')
- grad_out: bfloat16 [16, 256, 6144], P('pipe', None, 'fsdp')
All inputs are finite; a program needn't handle non-finite values.
Results may differ from a plain program's by a relative error of at most 0.035.
Values may be sent and summed in bfloat16 or wider, within the bound.
A program may use at most 64 MiB of HBM per device.

v0:
```python
import jax
import jax.numpy as jnp
from jax import lax
from jax.sharding import PartitionSpec as P

epsilon = 1e-06
root_half = 0.7071067811865476
inv_root_tau = 0.3989422804014327


def from_behind(shard, axis, by):
    length = lax.axis_size(axis)
    pairs = [(i, i + by) for i in range(length) if 0 <= i + by < length]
    return lax.ppermute(shard, axis, pairs)


def gelu_pair(preact):
    normal_cdf = 0.5 * (1.0 + lax.erf(preact * root_half))
    return (
        preact * normal_cdf,
        normal_cdf + preact * jnp.exp(-0.5 * preact * preact) * inv_root_tau,
    )


def normalize(hidden, gain_row):
    hidden_f32 = hidden.astype(jnp.float32)
    inverse = lax.rsqrt(jnp.mean(hidden_f32 * hidden_f32, axis=-1, keepdims=True) + epsilon)
    scaled = hidden_f32 * inverse
    return (hidden_f32, inverse, scaled, (scaled * gain_row).astype(jnp.bfloat16))


def forward_rows(hidden, weight_in, weight_out, gain_row):
    hidden_f32, inverse, scaled, normed = normalize(hidden, gain_row)
    preact = jnp.dot(normed, weight_in, preferred_element_type=jnp.float32)
    activated = gelu_pair(preact)[0].astype(jnp.bfloat16)
    branch = jnp.dot(activated, weight_out, preferred_element_type=jnp.float32)
    return (hidden_f32 + branch).astype(jnp.bfloat16)


def backward_rows(hidden, grad_next, weight_in, weight_out, gain_row):
    hidden_f32, inverse, scaled, normed = normalize(hidden, gain_row)
    preact = jnp.dot(normed, weight_in, preferred_element_type=jnp.float32)
    gelu_result, derivative = gelu_pair(preact)
    activated = gelu_result.astype(jnp.bfloat16)
    grad_act = jnp.dot(grad_next, weight_out.T, preferred_element_type=jnp.float32)
    grad_pre = (grad_act * derivative).astype(jnp.bfloat16)
    grad_normed = jnp.dot(grad_pre, weight_in.T, preferred_element_type=jnp.float32)
    grad_scaled = grad_normed * gain_row
    grad_path = inverse * (
        grad_scaled - scaled * jnp.mean(grad_scaled * scaled, axis=-1, keepdims=True)
    )
    grad_here = (grad_next.astype(jnp.float32) + grad_path).astype(jnp.bfloat16)
    return (grad_here, normed, activated, grad_pre)


def store_block(buffer, fresh, block_index, is_valid):
    previous = lax.dynamic_index_in_dim(buffer, block_index, 0, keepdims=False)
    return lax.dynamic_update_index_in_dim(
        buffer, jnp.where(is_valid, fresh, previous), block_index, 0
    )


def per_device(latents, upstream, proj_in, proj_out, norm_gain):
    section_count = lax.axis_size("pipe")
    section_index = lax.axis_index("pipe")
    micro_count, row_count, feature_count = latents.shape
    gathered = (
        lax.all_gather(proj_in, "fsdp", axis=1, tiled=True),
        lax.all_gather(proj_out, "fsdp", axis=2, tiled=True),
    )
    weight_in = gathered[0][0]
    weight_out = gathered[1][0]
    gain_row = norm_gain[0]
    inner_width = weight_in.shape[1]
    group_size = 1
    block_count = micro_count // group_size
    block_rows = group_size * row_count
    tick_count = block_count + section_count - 1
    blank = jnp.zeros((block_rows, feature_count), jnp.bfloat16)

    def forward_tick(current_tick, state_now):
        arrived_block, stash = state_now
        slot_index = current_tick - section_index
        is_valid = (slot_index >= 0) & (slot_index < block_count)
        block_index = jnp.clip(slot_index, 0, block_count - 1)
        first_rows = lax.dynamic_index_in_dim(latents, block_index, 0, keepdims=False)
        incoming = jnp.where(section_index == 0, first_rows, arrived_block)
        outgoing = forward_rows(incoming, weight_in, weight_out, gain_row)
        stash = store_block(stash, incoming, block_index, is_valid)
        return (from_behind(outgoing, "pipe", 1), stash)

    empty_stash = jnp.zeros((block_count, block_rows, feature_count), jnp.bfloat16)
    _, stash = lax.fori_loop(0, tick_count, forward_tick, (blank, empty_stash))

    def backward_tick(current_tick, state_now):
        arrived_block, normalized_saved, gradient_saved, activation_saved, preactivation_saved = (
            state_now
        )
        slot_index = current_tick - (section_count - 1 - section_index)
        is_valid = (slot_index >= 0) & (slot_index < block_count)
        block_index = jnp.clip(slot_index, 0, block_count - 1)
        last_grads = lax.dynamic_index_in_dim(upstream, block_index, 0, keepdims=False)
        grad_next = jnp.where(section_index == section_count - 1, last_grads, arrived_block)
        hidden = lax.dynamic_index_in_dim(stash, block_index, 0, keepdims=False)
        grad_here, normed, activated, grad_pre = backward_rows(
            hidden, grad_next, weight_in, weight_out, gain_row
        )
        normalized_saved = store_block(normalized_saved, normed, block_index, is_valid)
        gradient_saved = store_block(gradient_saved, grad_next, block_index, is_valid)
        activation_saved = store_block(activation_saved, activated, block_index, is_valid)
        preactivation_saved = store_block(preactivation_saved, grad_pre, block_index, is_valid)
        rotated_block = from_behind(grad_here, "pipe", -1)
        return (
            rotated_block,
            normalized_saved,
            gradient_saved,
            activation_saved,
            preactivation_saved,
        )

    narrow_store = jnp.zeros((block_count, block_rows, inner_width), jnp.bfloat16)
    final_state = lax.fori_loop(
        0, tick_count, backward_tick, (blank, empty_stash, empty_stash, narrow_store, narrow_store)
    )
    normalized_saved, gradient_saved, activation_saved, preactivation_saved = (
        final_state[1],
        final_state[2],
        final_state[3],
        final_state[4],
    )
    grad_in_part = jnp.einsum(
        "xiy,xih->yh", normalized_saved, preactivation_saved, preferred_element_type=jnp.float32
    )
    grad_out_part = jnp.einsum(
        "cvu,cvt->ut", activation_saved, gradient_saved, preferred_element_type=jnp.float32
    )
    reduced = (
        lax.psum_scatter(
            grad_in_part.astype(jnp.bfloat16), "fsdp", scatter_dimension=0, tiled=True
        ).astype(jnp.float32),
        lax.psum_scatter(
            grad_out_part.astype(jnp.bfloat16), "fsdp", scatter_dimension=1, tiled=True
        ).astype(jnp.float32),
    )
    return (reduced[0].astype(jnp.bfloat16)[None], reduced[1].astype(jnp.bfloat16)[None])


def solution(mesh):
    in_specs = (
        P(None, "fsdp", None),
        P(None, "fsdp", None),
        P("pipe", "fsdp", None),
        P("pipe", None, "fsdp"),
        P("pipe", None),
    )
    out_specs = (P("pipe", "fsdp", None), P("pipe", None, "fsdp"))
    return jax.shard_map(
        per_device, mesh=mesh, in_specs=in_specs, out_specs=out_specs, check_vma=False
    )
```

profile of v0, /device:TPU:2, one launch (start us, length us, event | category | flops | bytes accessed | tf_op | source)
XLA Modules:
  0.0 1259.6 jit_solution(18244800695235855544)
XLA Ops:
  8.7 74.9 %all-gather.3.cloned.1.call-done = bf16[1,6144,256]{2,1,0:T(8,128)(2,1)} async-done(((bf16[1,384,256]{2,1,0:T(8,128)(2,1)}), bf16[1,6144,256]{2,1,0:T(8,128)(2,1)}) %all-gather.3.cloned.1.call-update) | async-done | bytes 3145744 | tf_op jit(solution)/shard_map/all_gather | solution.py:68
  83.6 69.1 %all-gather.5.cloned.1.call-done = bf16[1,256,6144]{2,1,0:T(8,128)(2,1)} async-done(((bf16[1,256,384]{2,1,0:T(8,128)(2,1)}), bf16[1,256,6144]{2,1,0:T(8,128)(2,1)}) %all-gather.5.cloned.1.call-update) | async-done | bytes 3145744 | tf_op jit(solution)/shard_map/all_gather | solution.py:69
  154.7 404.5 %while.39 = (s32[]{:T(128)}, bf16[32,6144]{1,0:T(8,128)(2,1)}, bf16[4,32,6144]{2,1,0:T(8,128)(2,1)}, pred[]{:T(512)}, s32[]{:T(128)}, /*index=5*/bf16[4,32,6144]...) while((s32[]{:T(128)}, bf16[32,6144]{1,0:T(8,128)(2,1)}, ...), condition=%wide.region_2.3_spmd, body=%wide.region_0.2_spmd.sunk | while | flops 203726880 | bytes 25978144 | solution.py:93
  165.2 9.1 collective-permute-done
  564.0 484.5 %while.40 = (s32[]{:T(128)}, bf16[32,6144]{1,0:T(8,128)(2,1)}, bf16[4,32,6144]{2,1,0:T(8,128)(2,1)}, bf16[4,32,6144]{2,1,0:T(8,128)(2,1)}, bf16[4,32,256]{2,1,0:...) while((s32[]{:T(128)}, bf16[32,6144]{1,0:T(8,128)(2,1)}, ...), condition=%wide.region_6.7_spmd, body=%wide.region_3.6_spmd.sunk | while | flops 307437600 | bytes 41692972 | solution.py:122
  578.5 10.3 collective-permute-done.1
  604.0 10.9 collective-permute-done.1
  630.2 18.2 %collective-permute-done.1 = bf16[32,6144]{1,0:T(8,128)(2,1)S(1)} collective-permute-done((bf16[32,6144]{1,0:T(8,128)(2,1)}, bf16[32,6144]{1,0:T(8,128)(2,1)S(1)}, u32[]{:S(2)}, u32[]{:S(2)}) %collective-permute-start.1) | collective-permute-done | bytes 393248 | tf_op jit(solution)/shard_map/while/body/eval_jaxpr/ppermute | solution.py:14
  663.6 14.7 %collective-permute-done.1 = bf16[32,6144]{1,0:T(8,128)(2,1)S(1)} collective-permute-done((bf16[32,6144]{1,0:T(8,128)(2,1)}, bf16[32,6144]{1,0:T(8,128)(2,1)S(1)}, u32[]{:S(2)}, u32[]{:S(2)}) %collective-permute-start.1) | collective-permute-done | bytes 393248 | tf_op jit(solution)/shard_map/while/body/eval_jaxpr/ppermute | solution.py:14
  693.5 11.6 collective-permute-done.1
  720.4 9.9 collective-permute-done.1
  745.6 9.0 collective-permute-done.1
  817.6 9.2 collective-permute-done.1
  842.1 9.3 collective-permute-done.1
  866.6 9.3 collective-permute-done.1
  891.2 9.3 collective-permute-done.1
  915.7 9.3 collective-permute-done.1
  940.3 9.3 collective-permute-done.1
  964.8 9.2 collective-permute-done.1
  989.3 9.4 collective-permute-done.1
  1014.0 9.2 collective-permute-done.1
  1038.4 9.3 collective-permute-done.1
  1058.7 98.1 %reduce-scatter.7.cloned.1.call-done = bf16[384,256]{1,0:T(8,128)(2,1)} async-done(((bf16[6144,256]{1,0:T(8,128)(2,1)}), bf16[384,256]{1,0:T(8,128)(2,1)}) %reduce-scatter.7.cloned.1.call-update) | async-done | bytes 196624
  1158.5 94.6 %reduce-scatter.5.cloned.1.call-done = bf16[384,256]{1,0:T(8,128)(2,1)} async-done(((bf16[6144,256]{1,0:T(8,128)(2,1)}), bf16[384,256]{1,0:T(8,128)(2,1)}) %reduce-scatter.5.cloned.1.call-update) | async-done | bytes 196624 | tf_op jit(solution)/shard_map/reduce_scatter | solution.py:138
  (651 shorter events, 721.6 us)
Async XLA Ops:
  7.2 76.4 %all-gather.3.cloned.1.call-start = ((), (), s32[]{:S(2)}) async-start(), calls=%async_computation.2 | async-start | bytes 3342336 | tf_op jit(solution)/shard_map/all_gather | solution.py:68
  7.9 144.8 %all-gather.5.cloned.1.call-start = ((), (), s32[]{:S(2)}) async-start(), calls=%async_computation.3 | async-start | bytes 3342336 | tf_op jit(solution)/shard_map/all_gather | solution.py:69
  8.6 1148.1 %reduce-scatter.7.cloned.1.call-start = ((), (), s32[]{:S(2)}) async-start(), calls=%async_computation.5 | async-start | bytes 3342336
  182.9 12.7 %collective-permute-start = (bf16[32,6144]{1,0:T(8,128)(2,1)}, bf16[32,6144]{1,0:T(8,128)(2,1)S(1)}, u32[]{:S(2)}, u32[]{:S(2)}) collective-permute-start(bf16[32,6144]{1,0:T(8,128)(2,1)} %fusion.80), channel_id=1, source_target_pairs={{0,16},{16,32},{32,48},{48,64},{64,80},{80,96},{96,112},{112,128},... | collective-permute-start | bytes 1179656 | tf_op jit(solution)/shard_map/while/body/eval_jaxpr/ppermute | solution.py:14
  263.6 12.7 %collective-permute-start = (bf16[32,6144]{1,0:T(8,128)(2,1)}, bf16[32,6144]{1,0:T(8,128)(2,1)S(1)}, u32[]{:S(2)}, u32[]{:S(2)}) collective-permute-start(bf16[32,6144]{1,0:T(8,128)(2,1)} %fusion.80), channel_id=1, source_target_pairs={{0,16},{16,32},{32,48},{48,64},{64,80},{80,96},{96,112},{112,128},... | collective-permute-start | bytes 1179656 | tf_op jit(solution)/shard_map/while/body/eval_jaxpr/ppermute | solution.py:14
  306.2 12.7 %collective-permute-start = (bf16[32,6144]{1,0:T(8,128)(2,1)}, bf16[32,6144]{1,0:T(8,128)(2,1)S(1)}, u32[]{:S(2)}, u32[]{:S(2)}) collective-permute-start(bf16[32,6144]{1,0:T(8,128)(2,1)} %fusion.80), channel_id=1, source_target_pairs={{0,16},{16,32},{32,48},{48,64},{64,80},{80,96},{96,112},{112,128},... | collective-permute-start | bytes 1179656 | tf_op jit(solution)/shard_map/while/body/eval_jaxpr/ppermute | solution.py:14
  348.8 12.7 %collective-permute-start = (bf16[32,6144]{1,0:T(8,128)(2,1)}, bf16[32,6144]{1,0:T(8,128)(2,1)S(1)}, u32[]{:S(2)}, u32[]{:S(2)}) collective-permute-start(bf16[32,6144]{1,0:T(8,128)(2,1)} %fusion.80), channel_id=1, source_target_pairs={{0,16},{16,32},{32,48},{48,64},{64,80},{80,96},{96,112},{112,128},... | collective-permute-start | bytes 1179656 | tf_op jit(solution)/shard_map/while/body/eval_jaxpr/ppermute | solution.py:14
  370.2 12.7 %collective-permute-start = (bf16[32,6144]{1,0:T(8,128)(2,1)}, bf16[32,6144]{1,0:T(8,128)(2,1)S(1)}, u32[]{:S(2)}, u32[]{:S(2)}) collective-permute-start(bf16[32,6144]{1,0:T(8,128)(2,1)} %fusion.80), channel_id=1, source_target_pairs={{0,16},{16,32},{32,48},{48,64},{64,80},{80,96},{96,112},{112,128},... | collective-permute-start | bytes 1179656 | tf_op jit(solution)/shard_map/while/body/eval_jaxpr/ppermute | solution.py:14
  391.5 12.7 %collective-permute-start = (bf16[32,6144]{1,0:T(8,128)(2,1)}, bf16[32,6144]{1,0:T(8,128)(2,1)S(1)}, u32[]{:S(2)}, u32[]{:S(2)}) collective-permute-start(bf16[32,6144]{1,0:T(8,128)(2,1)} %fusion.80), channel_id=1, source_target_pairs={{0,16},{16,32},{32,48},{48,64},{64,80},{80,96},{96,112},{112,128},... | collective-permute-start | bytes 1179656 | tf_op jit(solution)/shard_map/while/body/eval_jaxpr/ppermute | solution.py:14
  412.8 12.7 %collective-permute-start = (bf16[32,6144]{1,0:T(8,128)(2,1)}, bf16[32,6144]{1,0:T(8,128)(2,1)S(1)}, u32[]{:S(2)}, u32[]{:S(2)}) collective-permute-start(bf16[32,6144]{1,0:T(8,128)(2,1)} %fusion.80), channel_id=1, source_target_pairs={{0,16},{16,32},{32,48},{48,64},{64,80},{80,96},{96,112},{112,128},... | collective-permute-start | bytes 1179656 | tf_op jit(solution)/shard_map/while/body/eval_jaxpr/ppermute | solution.py:14
  434.1 12.7 %collective-permute-start = (bf16[32,6144]{1,0:T(8,128)(2,1)}, bf16[32,6144]{1,0:T(8,128)(2,1)S(1)}, u32[]{:S(2)}, u32[]{:S(2)}) collective-permute-start(bf16[32,6144]{1,0:T(8,128)(2,1)} %fusion.80), channel_id=1, source_target_pairs={{0,16},{16,32},{32,48},{48,64},{64,80},{80,96},{96,112},{112,128},... | collective-permute-start | bytes 1179656 | tf_op jit(solution)/shard_map/while/body/eval_jaxpr/ppermute | solution.py:14
  455.4 12.7 %collective-permute-start = (bf16[32,6144]{1,0:T(8,128)(2,1)}, bf16[32,6144]{1,0:T(8,128)(2,1)S(1)}, u32[]{:S(2)}, u32[]{:S(2)}) collective-permute-start(bf16[32,6144]{1,0:T(8,128)(2,1)} %fusion.80), channel_id=1, source_target_pairs={{0,16},{16,32},{32,48},{48,64},{64,80},{80,96},{96,112},{112,128},... | collective-permute-start | bytes 1179656 | tf_op jit(solution)/shard_map/while/body/eval_jaxpr/ppermute | solution.py:14
  476.8 12.7 %collective-permute-start = (bf16[32,6144]{1,0:T(8,128)(2,1)}, bf16[32,6144]{1,0:T(8,128)(2,1)S(1)}, u32[]{:S(2)}, u32[]{:S(2)}) collective-permute-start(bf16[32,6144]{1,0:T(8,128)(2,1)} %fusion.80), channel_id=1, source_target_pairs={{0,16},{16,32},{32,48},{48,64},{64,80},{80,96},{96,112},{112,128},... | collective-permute-start | bytes 1179656 | tf_op jit(solution)/shard_map/while/body/eval_jaxpr/ppermute | solution.py:14
  498.1 14.1 %collective-permute-start = (bf16[32,6144]{1,0:T(8,128)(2,1)}, bf16[32,6144]{1,0:T(8,128)(2,1)S(1)}, u32[]{:S(2)}, u32[]{:S(2)}) collective-permute-start(bf16[32,6144]{1,0:T(8,128)(2,1)} %fusion.80), channel_id=1, source_target_pairs={{0,16},{16,32},{32,48},{48,64},{64,80},{80,96},{96,112},{112,128},... | collective-permute-start | bytes 1179656 | tf_op jit(solution)/shard_map/while/body/eval_jaxpr/ppermute | solution.py:14
  520.8 15.5 %collective-permute-start = (bf16[32,6144]{1,0:T(8,128)(2,1)}, bf16[32,6144]{1,0:T(8,128)(2,1)S(1)}, u32[]{:S(2)}, u32[]{:S(2)}) collective-permute-start(bf16[32,6144]{1,0:T(8,128)(2,1)} %fusion.80), channel_id=1, source_target_pairs={{0,16},{16,32},{32,48},{48,64},{64,80},{80,96},{96,112},{112,128},... | collective-permute-start | bytes 1179656 | tf_op jit(solution)/shard_map/while/body/eval_jaxpr/ppermute | solution.py:14
  544.9 13.6 %collective-permute-start = (bf16[32,6144]{1,0:T(8,128)(2,1)}, bf16[32,6144]{1,0:T(8,128)(2,1)S(1)}, u32[]{:S(2)}, u32[]{:S(2)}) collective-permute-start(bf16[32,6144]{1,0:T(8,128)(2,1)} %fusion.80), channel_id=1, source_target_pairs={{0,16},{16,32},{32,48},{48,64},{64,80},{80,96},{96,112},{112,128},... | collective-permute-start | bytes 1179656 | tf_op jit(solution)/shard_map/while/body/eval_jaxpr/ppermute | solution.py:14
  575.2 13.5 %collective-permute-start.1 = (bf16[32,6144]{1,0:T(8,128)(2,1)}, bf16[32,6144]{1,0:T(8,128)(2,1)S(1)}, u32[]{:S(2)}, u32[]{:S(2)}) collective-permute-start(bf16[32,6144]{1,0:T(8,128)(2,1)} %fusion.89), channel_id=1, source_target_pairs={{16,0},{32,16},{48,32},{64,48},{80,64},{96,80},{112,96},{128,112},... | collective-permute-start | bytes 1179656 | tf_op jit(solution)/shard_map/while/body/eval_jaxpr/ppermute | solution.py:14
  600.8 14.1 %collective-permute-start.1 = (bf16[32,6144]{1,0:T(8,128)(2,1)}, bf16[32,6144]{1,0:T(8,128)(2,1)S(1)}, u32[]{:S(2)}, u32[]{:S(2)}) collective-permute-start(bf16[32,6144]{1,0:T(8,128)(2,1)} %fusion.89), channel_id=1, source_target_pairs={{16,0},{32,16},{48,32},{64,48},{80,64},{96,80},{112,96},{128,112},... | collective-permute-start | bytes 1179656 | tf_op jit(solution)/shard_map/while/body/eval_jaxpr/ppermute | solution.py:14
  626.9 21.5 %collective-permute-start.1 = (bf16[32,6144]{1,0:T(8,128)(2,1)}, bf16[32,6144]{1,0:T(8,128)(2,1)S(1)}, u32[]{:S(2)}, u32[]{:S(2)}) collective-permute-start(bf16[32,6144]{1,0:T(8,128)(2,1)} %fusion.89), channel_id=1, source_target_pairs={{16,0},{32,16},{48,32},{64,48},{80,64},{96,80},{112,96},{128,112},... | collective-permute-start | bytes 1179656 | tf_op jit(solution)/shard_map/while/body/eval_jaxpr/ppermute | solution.py:14
  660.3 17.9 %collective-permute-start.1 = (bf16[32,6144]{1,0:T(8,128)(2,1)}, bf16[32,6144]{1,0:T(8,128)(2,1)S(1)}, u32[]{:S(2)}, u32[]{:S(2)}) collective-permute-start(bf16[32,6144]{1,0:T(8,128)(2,1)} %fusion.89), channel_id=1, source_target_pairs={{16,0},{32,16},{48,32},{64,48},{80,64},{96,80},{112,96},{128,112},... | collective-permute-start | bytes 1179656 | tf_op jit(solution)/shard_map/while/body/eval_jaxpr/ppermute | solution.py:14
  690.3 14.9 %collective-permute-start.1 = (bf16[32,6144]{1,0:T(8,128)(2,1)}, bf16[32,6144]{1,0:T(8,128)(2,1)S(1)}, u32[]{:S(2)}, u32[]{:S(2)}) collective-permute-start(bf16[32,6144]{1,0:T(8,128)(2,1)} %fusion.89), channel_id=1, source_target_pairs={{16,0},{32,16},{48,32},{64,48},{80,64},{96,80},{112,96},{128,112},... | collective-permute-start | bytes 1179656 | tf_op jit(solution)/shard_map/while/body/eval_jaxpr/ppermute | solution.py:14
  717.1 13.2 %collective-permute-start.1 = (bf16[32,6144]{1,0:T(8,128)(2,1)}, bf16[32,6144]{1,0:T(8,128)(2,1)S(1)}, u32[]{:S(2)}, u32[]{:S(2)}) collective-permute-start(bf16[32,6144]{1,0:T(8,128)(2,1)} %fusion.89), channel_id=1, source_target_pairs={{16,0},{32,16},{48,32},{64,48},{80,64},{96,80},{112,96},{128,112},... | collective-permute-start | bytes 1179656 | tf_op jit(solution)/shard_map/while/body/eval_jaxpr/ppermute | solution.py:14
  986.0 12.7 %collective-permute-start.1 = (bf16[32,6144]{1,0:T(8,128)(2,1)}, bf16[32,6144]{1,0:T(8,128)(2,1)S(1)}, u32[]{:S(2)}, u32[]{:S(2)}) collective-permute-start(bf16[32,6144]{1,0:T(8,128)(2,1)} %fusion.89), channel_id=1, source_target_pairs={{16,0},{32,16},{48,32},{64,48},{80,64},{96,80},{112,96},{128,112},... | collective-permute-start | bytes 1179656 | tf_op jit(solution)/shard_map/while/body/eval_jaxpr/ppermute | solution.py:14
  1053.8 199.3 %reduce-scatter.5.cloned.1.call-start = ((), (), s32[]{:S(2)}) async-start(), calls=%async_computation.4 | async-start | bytes 3342336 | tf_op jit(solution)/shard_map/reduce_scatter | solution.py:138
  (153 other events, 508.8 us)
Sparse Core Ops, SparseCore 0:
  10.7 72.8 all-gather.2
  86.2 66.4 all-gather.4
  1053.9 102.8 reduce-scatter.6
  1161.5 91.5 reduce-scatter.4
where the time goes:
time: 1270 us; the launch traced here: 1260 us
  waiting for transfers between devices  651 us (51%)
  matrix products  193 us (15%)
  other arithmetic  157 us (12%)
  starting transfers between devices  147 us (12%)
  local copies, waits for them, and re-layouts  97.3 us (8%)
  between operations  13.8 us (1%)
    ppermute x38, waiting for transfers between devices, from_behind(): return lax.ppermute(shard, axis, pairs)  313 us
    ppermute x38, starting transfers between devices, from_behind(): return lax.ppermute(shard, axis, pairs)  147 us
    dynamic_update_slice x57, other arithmetic, store_block(): lax.dynamic_update_index_in_dim(buffer, jnp.where(is_valid, fresh, previo...  111 us
    unnamed x5, waiting for transfers between devices  99.5 us
    reduce_scatter x1, waiting for transfers between devices, per_device(): lax.psum_scatter(grad_in_part.astype(jnp.bfloat16), 'fsdp', scatter_dimen...  94.6 us
    dot_general x19, matrix products, forward_rows(): branch = jnp.dot(activated, weight_out, preferred_element_type=jnp.float32)  86.5 us
    all_gather x1, waiting for transfers between devices, per_device(): lax.all_gather(proj_in, 'fsdp', axis=1, tiled=True)  74.9 us
    all_gather x1, waiting for transfers between devices, per_device(): lax.all_gather(proj_out, 'fsdp', axis=2, tiled=True)  69.1 us
  transfers between devices with their start and end apart: 42, of which 42 were waited for; matrix products, arithmetic and copies ran while one was open for 3% of the time, Pallas kernels for 0%

commit v1 on v0

v1 whole, which is shorter than its diff:
```python
import functools

import jax
import jax.numpy as jnp
from jax import lax
from jax.experimental import pallas as pl
from jax.experimental.pallas import tpu as pltpu
from jax.sharding import PartitionSpec as P

MESH = pl.DeviceIdType.MESH
epsilon = 1e-06
root_half = 0.7071067811865476
inv_root_tau = 0.3989422804014327
ROWS = 16
CHUNKS = 3


def relay_kernel(
    stages, blocks, features,
    lat_ref, up_ref, win_ref, wout_ref, pin_ref, pout_ref,
    h_in, h_out, g_in, g_out, act_s, slope_s, pre_s, inv_s, q_s,
    f_send, f_recv, b_send, b_recv,
):
    s = lax.axis_index("pipe")
    f = lax.axis_index("fsdp")
    wide = features // CHUNKS
    after = lax.rem(s + 1, stages)
    before = lax.rem(s + stages - 1, stages)

    barrier = pltpu.get_barrier_semaphore()
    for other in (before, after):
        pl.semaphore_signal(barrier, inc=1, device_id=(other, f), device_id_type=MESH)
    pl.semaphore_wait(barrier, 2)

    def columns(c):
        return pl.ds(c * wide, wide)

    def f_copy(i, c):
        return pltpu.make_async_remote_copy(
            src_ref=h_out.at[i, :, columns(c)], dst_ref=h_in.at[i, :, columns(c)],
            send_sem=f_send.at[i, c], recv_sem=f_recv.at[i, c],
            device_id=(after, f), device_id_type=MESH,
        )

    def b_copy(i, c):
        return pltpu.make_async_remote_copy(
            src_ref=g_out.at[i, :, columns(c)], dst_ref=g_in.at[i, :, columns(c)],
            send_sem=b_send.at[i, c], recv_sem=b_recv.at[i, c],
            device_id=(before, f), device_id_type=MESH,
        )

    @pl.when(s == 0)
    def _():
        @pl.loop(0, blocks)
        def _(i):
            for c in range(CHUNKS):
                pltpu.make_async_copy(
                    lat_ref.at[i, :, columns(c)], h_in.at[i, :, columns(c)], f_recv.at[i, c]
                ).start()

    @pl.when(s == stages - 1)
    def _():
        @pl.loop(0, blocks)
        def _(i):
            for c in range(CHUNKS):
                pltpu.make_async_copy(
                    up_ref.at[i, :, columns(c)], g_in.at[i, :, columns(c)], b_recv.at[i, c]
                ).start()

    def forward(i):
        pre = jnp.zeros((ROWS, win_ref.shape[1]), jnp.float32)
        square = jnp.zeros((ROWS, 1), jnp.float32)
        for c in range(CHUNKS):
            f_copy(i, c).wait_recv()
            h = h_in[i, :, columns(c)]
            pre += jnp.dot(h, win_ref[columns(c), :], preferred_element_type=jnp.float32)
            wide_h = h.astype(jnp.float32)
            square += jnp.sum(wide_h * wide_h, axis=-1, keepdims=True)
        inverse = lax.rsqrt(square * (1.0 / features) + epsilon)
        pre = pre * inverse
        cdf = 0.5 * (1.0 + lax.erf(pre * root_half))
        act = (pre * cdf).astype(jnp.bfloat16)

        @pl.when(s < stages - 1)
        def _():
            for c in range(CHUNKS):
                branch = jnp.dot(act, wout_ref[:, columns(c)], preferred_element_type=jnp.float32)
                h_out[i, :, columns(c)] = (
                    h_in[i, :, columns(c)].astype(jnp.float32) + branch
                ).astype(jnp.bfloat16)
                f_copy(i, c).start()

        act_s[i] = act
        pre_s[i] = pre
        slope_s[i] = cdf + pre * jnp.exp(-0.5 * pre * pre) * inv_root_tau
        inv_s[i] = jnp.broadcast_to(inverse, pre.shape)

    def backward(i):
        grad_act = jnp.zeros((ROWS, win_ref.shape[1]), jnp.float32)
        for c in range(CHUNKS):
            b_copy(i, c).wait_recv()
            grad_act += lax.dot_general(
                g_in[i, :, columns(c)], wout_ref[:, columns(c)], (((1,), (1,)), ((), ())),
                preferred_element_type=jnp.float32,
            )
        grad_pre = grad_act * slope_s[i]
        inverse = inv_s[i]
        mean = jnp.sum(grad_pre * pre_s[i], axis=-1, keepdims=True) * (1.0 / features)
        q = (grad_pre * inverse).astype(jnp.bfloat16)
        q_s[i] = q
        pull = inverse[:, :1] * inverse[:, :1] * mean

        @pl.when(s > 0)
        def _():
            for c in range(CHUNKS):
                path = lax.dot_general(
                    q, win_ref[columns(c), :], (((1,), (1,)), ((), ())),
                    preferred_element_type=jnp.float32,
                )
                g_out[i, :, columns(c)] = (
                    g_in[i, :, columns(c)].astype(jnp.float32) + path
                    - pull * h_in[i, :, columns(c)].astype(jnp.float32)
                ).astype(jnp.bfloat16)
                b_copy(i, c).start()

    @pl.loop(0, blocks + 2 * stages - 2)
    def _(tick):
        ahead = tick - s
        back = tick - (2 * stages - 2) + s

        @pl.when((ahead >= 0) & (ahead < blocks))
        def _():
            forward(ahead)

        @pl.when((back >= 0) & (back < blocks))
        def _():
            backward(back)

    tokens = blocks * ROWS
    part = 512
    q_all = q_s[...].reshape(tokens, -1)
    act_all = act_s[...].reshape(tokens, -1)

    @pl.loop(0, features // part)
    def _(n):
        cut = pl.ds(pl.multiple_of(n * part, part), part)
        h = h_in[:, :, cut].reshape(tokens, part)
        pin_ref[cut, :] = lax.dot_general(
            h, q_all, (((0,), (0,)), ((), ())), preferred_element_type=jnp.float32
        ).astype(jnp.bfloat16)
        g = g_in[:, :, cut].reshape(tokens, part)
        pout_ref[:, cut] = lax.dot_general(
            act_all, g, (((0,), (0,)), ((), ())), preferred_element_type=jnp.float32
        ).astype(jnp.bfloat16)

    @pl.when(s < stages - 1)
    def _():
        @pl.loop(0, blocks)
        def _(i):
            for c in range(CHUNKS):
                f_copy(i, c).wait_send()

    @pl.when(s > 0)
    def _():
        @pl.loop(0, blocks)
        def _(i):
            for c in range(CHUNKS):
                b_copy(i, c).wait_send()


def per_device(latents, upstream, proj_in, proj_out, norm_gain):
    stages = lax.axis_size("pipe")
    shards = lax.axis_size("fsdp")
    f = lax.axis_index("fsdp")
    features = latents.shape[2]
    inner = proj_in.shape[2]
    share = features // shards
    gain = lax.dynamic_slice_in_dim(norm_gain[0], f * share, share)[:, None]
    scaled_in = (proj_in[0].astype(jnp.float32) * gain).astype(jnp.bfloat16)
    weight_in = lax.all_gather(scaled_in, "fsdp", axis=0, tiled=True)
    weight_out = lax.all_gather(proj_out[0], "fsdp", axis=1, tiled=True)
    blocks = latents.shape[0] * latents.shape[1] // ROWS
    lat = latents.reshape(blocks, ROWS, features)
    up = upstream.reshape(blocks, ROWS, features)
    vmem = pl.BlockSpec(memory_space=pltpu.VMEM)
    anywhere = pl.BlockSpec(memory_space=pl.ANY)
    wide_buffer = pltpu.VMEM((blocks, ROWS, features), jnp.bfloat16)
    narrow = pltpu.VMEM((blocks, ROWS, inner), jnp.bfloat16)
    narrow_f32 = pltpu.VMEM((blocks, ROWS, inner), jnp.float32)
    sems = pltpu.SemaphoreType.DMA((blocks, CHUNKS))
    part_in, part_out = pl.pallas_call(
        functools.partial(relay_kernel, stages, blocks, features),
        out_shape=(
            jax.ShapeDtypeStruct((features, inner), jnp.bfloat16),
            jax.ShapeDtypeStruct((inner, features), jnp.bfloat16),
        ),
        in_specs=[anywhere, anywhere, vmem, vmem],
        out_specs=(vmem, vmem),
        scratch_shapes=[
            wide_buffer, wide_buffer, wide_buffer, wide_buffer,
            narrow, narrow_f32, narrow_f32, narrow_f32, narrow,
            sems, sems, sems, sems,
        ],
        compiler_params=pltpu.CompilerParams(
            collective_id=0, has_side_effects=True, vmem_limit_bytes=48 * 1024 * 1024
        ),
        name="relay",
    )(lat, up, weight_in, weight_out)
    grad_in = lax.psum_scatter(part_in, "fsdp", scatter_dimension=0, tiled=True)
    grad_out = lax.psum_scatter(part_out, "fsdp", scatter_dimension=1, tiled=True)
    grad_in = (grad_in.astype(jnp.float32) * gain).astype(jnp.bfloat16)
    return grad_in[None], grad_out[None]


def solution(mesh):
    in_specs = (
        P(None, "fsdp", None),
        P(None, "fsdp", None),
        P("pipe", "fsdp", None),
        P("pipe", None, "fsdp"),
        P("pipe", None),
    )
    out_specs = (P("pipe", "fsdp", None), P("pipe", None, "fsdp"))
    return jax.shard_map(
        per_device, mesh=mesh, in_specs=in_specs, out_specs=out_specs, check_vma=False
    )
```

time: 1270 us -> 614 us (0.48)
  waiting for transfers between devices: 651 us -> 327 us
  Pallas kernels: 0 us -> 260 us
  matrix products: 193 us -> 0 us
  other arithmetic: 157 us -> 3.44 us
  starting transfers between devices: 147 us -> 0.16 us
  local copies, waits for them, and re-layouts: 97.3 us -> 9.31 us
    ppermute x38 -> x0, waiting for transfers between devices: 313 us -> none  [from_behind(): return lax.ppermute(shard, axis, pairs)]
    pallas_call x0 -> x1, Pallas kernels: none -> 260 us  [per_device(): pl.pallas_call(functools.partial(relay_kernel, stages, blocks, features),...]
    dot_general x78 -> x0, matrix products: 193 us -> none  [the longest x19 86.5 us: forward_rows(): branch = jnp.dot(activated, weight_out, preferred_element_type=jnp.float32)]
    ppermute x38 -> x0, starting transfers between devices: 147 us -> none  [from_behind(): return lax.ppermute(shard, axis, pairs)]
    dynamic_update_slice x57 -> x0, other arithmetic: 111 us -> none  [store_block(): lax.dynamic_update_index_in_dim(buffer, jnp.where(is_valid, fresh, previo...]
    dynamic_slice x57 -> x1, local copies, waits for them, and re-layouts: 56 us -> 0.02 us  [per_device(): gain = lax.dynamic_slice_in_dim(norm_gain[0], f * share, share)[:, None]]
    while x266 -> x0, local copies, waits for them, and re-layouts: 29.1 us -> none
    reduce_sum x38 -> x0, other arithmetic: 26.3 us -> none  [normalize(): jnp.mean(hidden_f32 * hidden_f32, axis=-1, keepdims=True) + epsilon]
  transfers between devices with their start and end apart: 42 -> 4, of which waited for: 42 -> 4; matrix products, arithmetic and copies ran while one was open for 3% -> 1% of each run, Pallas kernels for 0% -> 0%
where the time goes in v1:
time: 614 us
  waiting for transfers between devices  327 us (53%)
  Pallas kernels  260 us (42%)
  between operations  13.8 us (2%)
  local copies, waits for them, and re-layouts  9.31 us (2%)
    pallas_call x1, Pallas kernels, per_device(): pl.pallas_call(functools.partial(relay_kernel, stages, blocks, features),...  260 us
    reduce_scatter x1, waiting for transfers between devices, per_device(): grad_in = lax.psum_scatter(part_in, 'fsdp', scatter_dimension=0, tiled=True)  94 us
    unnamed x5, waiting for transfers between devices  89 us
    all_gather x1, waiting for transfers between devices, per_device(): weight_out = lax.all_gather(proj_out[0], 'fsdp', axis=1, tiled=True)  74.1 us
    all_gather x1, waiting for transfers between devices, per_device(): weight_in = lax.all_gather(scaled_in, 'fsdp', axis=0, tiled=True)  69.7 us
  transfers between devices with their start and end apart: 4, of which 4 were waited for; matrix products, arithmetic and copies ran while one was open for 1% of the time, Pallas kernels for 0%

profile of v1, /device:TPU:2, one launch (start us, length us, event | category | flops | bytes accessed | tf_op | source)
XLA Modules:
  0.0 613.7 jit_solution(10468676538028791088)
XLA Ops:
  7.2 0.0 copy-start
  7.2 0.0 all-gather.6.cloned.1.call-start
  7.2 0.7 all-gather.6.cloned.1.call-update
  7.9 0.0 all-gather.4.cloned.1.call-start
  8.0 0.0 copy-done
  8.0 1.7 fusion
  9.7 0.0 all-gather.4.cloned.1.call-update
  9.7 0.0 reduce-scatter.7.cloned.1.call-start
  9.8 74.1 %all-gather.6.cloned.1.call-done = bf16[1,256,6144]{2,1,0:T(8,128)(2,1)} async-done(((bf16[1,256,384]{2,1,0:T(8,128)(2,1)}), bf16[1,256,6144]{2,1,0:T(8,128)(2,1)}) %all-gather.6.cloned.1.call-update) | async-done | bytes 3145744 | tf_op jit(solution)/shard_map/all_gather | solution.py:181
  83.9 69.7 %all-gather.4.cloned.1.call-done.win_ref = bf16[6144,256]{1,0:T(8,128)(2,1)} async-done(((bf16[384,256]{1,0:T(8,128)(2,1)}), bf16[6144,256]{1,0:T(8,128)(2,1)}) %all-gather.4.cloned.1.call-update) | async-done | bytes 3145744 | tf_op jit(solution)/shard_map/all_gather | solution.py:180
  153.6 0.0 copy-start.1
  153.6 1.4 copy-done.1
  155.0 0.0 copy-start.2
  155.0 1.4 copy-done.2
  156.4 260.2 %relay.1 = (bf16[6144,256]{1,0:T(8,128)(2,1)}, bf16[256,6144]{1,0:T(8,128)(2,1)}) custom-call(bf16[8,16,6144]{2,1,0:T(8,128)(2,1)S(1)} %bitcast.11, bf16[8,16,6144]{2,1,0:T(8,128)(2,1)S(1)} %bitcast.12, bf16[6144,256]{1,0:T(8,128)(2,1)} %all-gather.4.cloned.1.call-done.win_ref, bf16[256,6144]{1,0:T(8,128)(2,1)} %bitcast.14), custom_call_target="tpu_custom_call" | custom-call | tf_op jit(solution)/shard_map/relay/pallas_call | solution.py:191
  416.6 4.7 copy.7
  421.3 0.0 reduce-scatter.7.cloned.1.call-update
  421.3 0.0 reduce-scatter.5.cloned.1.call-start
  421.4 0.5 reduce-scatter.5.cloned.1.call-update
  421.9 87.8 %reduce-scatter.7.cloned.1.call-done = bf16[384,256]{1,0:T(8,128)(2,1)} async-done(((bf16[6144,256]{1,0:T(8,128)(2,1)}), bf16[384,256]{1,0:T(8,128)(2,1)}) %reduce-scatter.7.cloned.1.call-update) | async-done | bytes 196624
  509.7 1.7 copy.8
  511.4 94.0 %reduce-scatter.5.cloned.1.call-done = bf16[384,256]{1,0:T(8,128)(2,1)} async-done(((bf16[6144,256]{1,0:T(8,128)(2,1)}), bf16[384,256]{1,0:T(8,128)(2,1)}) %reduce-scatter.5.cloned.1.call-update) | async-done | bytes 196624 | tf_op jit(solution)/shard_map/reduce_scatter | solution.py:209
  605.4 1.7 fusion.1
  (1 shorter events, 0.0 us)
Async XLA Ops:
  7.2 0.8 copy-start
  7.2 76.7 %all-gather.6.cloned.1.call-start = ((), (), s32[]{:S(2)}) async-start(), calls=%async_computation.4 | async-start | bytes 3342336 | tf_op jit(solution)/shard_map/all_gather | solution.py:181
  7.9 145.7 %all-gather.4.cloned.1.call-start = ((), (), s32[]{:S(2)}) async-start(), calls=%async_computation.2 | async-start | bytes 3342336 | tf_op jit(solution)/shard_map/all_gather | solution.py:180
  9.7 499.9 %reduce-scatter.7.cloned.1.call-start = ((), (), s32[]{:S(2)}) async-start(), calls=%async_computation.5 | async-start | bytes 3342336
  153.6 1.4 copy-start.1
  155.0 1.4 copy-start.2
  421.3 184.1 %reduce-scatter.5.cloned.1.call-start = ((), (), s32[]{:S(2)}) async-start(), calls=%async_computation.3 | async-start | bytes 3342336 | tf_op jit(solution)/shard_map/reduce_scatter | solution.py:209
Sparse Core Ops, SparseCore 0:
  10.6 73.2 all-gather.5
  87.2 66.3 all-gather.3
  421.5 88.1 reduce-scatter.6
  513.9 91.5 reduce-scatter.4

commit v2 on v1

--- a/solution.py
+++ b/solution.py
@@ -17,20 +17,72 @@
 
 def relay_kernel(
     stages, blocks, features,
-    lat_ref, up_ref, win_ref, wout_ref, pin_ref, pout_ref,
+    lat_ref, up_ref, pin_ref, pout_ref, gain_ref, gin_ref, gout_ref,
+    win_ref, wout_ref,
     h_in, h_out, g_in, g_out, act_s, slope_s, pre_s, inv_s, q_s,
-    f_send, f_recv, b_send, b_recv,
+    pair_in, pair_out, pair_in_stage, pair_out_stage,
+    ring_in, ring_out, ring_in_stage, ring_out_stage,
+    far_in, far_out, far_in_stage, far_out_stage, sum_in, sum_out,
+    f_send, f_recv, b_send, b_recv, ag_send, ag_recv,
+    pair_send, pair_recv, ring_send, ring_recv, far_send, far_recv,
 ):
     s = lax.axis_index("pipe")
     f = lax.axis_index("fsdp")
     wide = features // CHUNKS
+    share = pin_ref.shape[0]
     after = lax.rem(s + 1, stages)
     before = lax.rem(s + stages - 1, stages)
+    half = f // 8
+    place = lax.rem(f, 8) // 2
+    core = lax.rem(f, 2)
+
+    def index_of(z, x, c):
+        return z * 8 + lax.rem(x + 4, 4) * 2 + c
+
+    right = index_of(half, place + 1, core)
+    left = index_of(half, place - 1, core)
+    pair = index_of(half, place, 1 - core)
+    far = index_of(1 - half, place, core)
 
     barrier = pltpu.get_barrier_semaphore()
-    for other in (before, after):
-        pl.semaphore_signal(barrier, inc=1, device_id=(other, f), device_id_type=MESH)
-    pl.semaphore_wait(barrier, 2)
+    for other in ((before, f), (after, f), (s, right), (s, left), (s, pair), (s, far)):
+        pl.semaphore_signal(barrier, inc=1, device_id=other, device_id_type=MESH)
+
+    def rows_of(j):
+        return pl.ds(pl.multiple_of(j * share, 128), share)
+
+    win_ref[rows_of(f), :] = (pin_ref[...].astype(jnp.float32) * gain_ref[...]).astype(jnp.bfloat16)
+    wout_ref[:, rows_of(f)] = pout_ref[...]
+    pl.semaphore_wait(barrier, 6)
+
+    routes = (far, right, left, pair)
+
+    def shard(j, piece):
+        return win_ref.at[rows_of(j), :] if piece == 0 else wout_ref.at[:, rows_of(j)]
+
+    def spread(j, piece, route):
+        return pltpu.make_async_remote_copy(
+            src_ref=shard(j, piece), dst_ref=shard(j, piece),
+            send_sem=ag_send.at[route, j, piece], recv_sem=ag_recv.at[j, piece],
+            device_id=(s, routes[route]), device_id_type=MESH,
+        )
+
+    sent = []
+
+    def share_out(j, piece, *ways):
+        for way in ways:
+            spread(j, piece, way).start()
+            sent.append((j, piece, way))
+
+    def arrived(j, piece):
+        spread(j, piece, 3).wait_recv()
+
+    for piece in (0, 1):
+        share_out(f, piece, 0)
+    for piece in (0, 1):
+        share_out(f, piece, 1, 2)
+    for piece in (0, 1):
+        share_out(f, piece, 3)
 
     def columns(c):
         return pl.ds(c * wide, wide)
@@ -67,6 +119,27 @@
                     up_ref.at[i, :, columns(c)], g_in.at[i, :, columns(c)], b_recv.at[i, c]
                 ).start()
 
+    for z in (half, 1 - half):
+        mine, on_left, on_right, across = [index_of(z, place + step, core) for step in (0, -1, 1, 2)]
+        if z is not half:
+            for piece in (0, 1):
+                arrived(mine, piece)
+                share_out(mine, piece, 1, 2, 3)
+        arrived(on_left, 0)
+        share_out(on_left, 0, 1, 3)
+        arrived(on_right, 0)
+        share_out(on_right, 0, 3)
+        arrived(on_right, 1)
+        share_out(on_right, 1, 2, 3)
+        arrived(on_left, 1)
+        share_out(on_left, 1, 3)
+        for piece in (0, 1):
+            arrived(across, piece)
+            share_out(across, piece, 3)
+    for z in (half, 1 - half):
+        for step in (0, -1, 1, 2):
+            for piece in (0, 1):
+                arrived(index_of(z, place + step, 1 - core), piece)
     def forward(i):
         pre = jnp.zeros((ROWS, win_ref.shape[1]), jnp.float32)
         square = jnp.zeros((ROWS, 1), jnp.float32)
@@ -137,21 +210,108 @@
             backward(back)
 
     tokens = blocks * ROWS
-    part = 512
     q_all = q_s[...].reshape(tokens, -1)
     act_all = act_s[...].reshape(tokens, -1)
-
-    @pl.loop(0, features // part)
-    def _(n):
-        cut = pl.ds(pl.multiple_of(n * part, part), part)
-        h = h_in[:, :, cut].reshape(tokens, part)
-        pin_ref[cut, :] = lax.dot_general(
-            h, q_all, (((0,), (0,)), ((), ())), preferred_element_type=jnp.float32
-        ).astype(jnp.bfloat16)
-        g = g_in[:, :, cut].reshape(tokens, part)
-        pout_ref[:, cut] = lax.dot_general(
-            act_all, g, (((0,), (0,)), ((), ())), preferred_element_type=jnp.float32
-        ).astype(jnp.bfloat16)
+    over_tokens = (((0,), (0,)), ((), ()))
+
+    def part_in(j):
+        h = h_in[:, :, rows_of(j)].reshape(tokens, share)
+        return lax.dot_general(h, q_all, over_tokens, preferred_element_type=jnp.float32)
+
+    def part_out(j):
+        g = g_in[:, :, rows_of(j)].reshape(tokens, share)
+        return lax.dot_general(act_all, g, over_tokens, preferred_element_type=jnp.float32)
+
+    def remote(src, dst, send, recv, route):
+        return pltpu.make_async_remote_copy(
+            src_ref=src, dst_ref=dst, send_sem=send, recv_sem=recv,
+            device_id=(s, routes[route]), device_id_type=MESH,
+        )
+
+    def pair_copy(m, piece):
+        stage, land = ((pair_in_stage, pair_in), (pair_out_stage, pair_out))[piece]
+        return remote(stage.at[m], land.at[m], pair_send.at[m, piece], pair_recv.at[m, piece], 3)
+
+    def ring_copy(h, slot, piece):
+        stage, land = ((ring_in_stage, ring_in), (ring_out_stage, ring_out))[piece]
+        way = 1 if (slot == 2) == (piece == 1) else 2
+        return remote(
+            stage.at[h, slot], land.at[h, slot],
+            ring_send.at[h, slot, piece], ring_recv.at[h, slot, piece], way,
+        )
+
+    def far_copy(piece):
+        stage, land = ((far_in_stage, far_in), (far_out_stage, far_out))[piece]
+        return remote(stage, land, far_send.at[piece], far_recv.at[piece], 0)
+
+    steps = (2, 1, -1, 0)
+    halves = (1 - half, half)
+    for h in (0, 1):
+        for k, step in enumerate(steps):
+            m = h * 4 + k
+            j = index_of(halves[h], place + step, 1 - core)
+            pair_in_stage[m] = part_in(j).astype(jnp.bfloat16)
+            pair_copy(m, 0).start()
+            pair_out_stage[m] = part_out(j).astype(jnp.bfloat16)
+            pair_copy(m, 1).start()
+
+    def both_in(h, k):
+        pair_copy(h * 4 + k, 0).wait_recv()
+        j = index_of(halves[h], place + steps[k], core)
+        return part_in(j) + pair_in[h * 4 + k].astype(jnp.float32)
+
+    def both_out(h, k):
+        pair_copy(h * 4 + k, 1).wait_recv()
+        j = index_of(halves[h], place + steps[k], core)
+        return part_out(j) + pair_out[h * 4 + k].astype(jnp.float32)
+
+    for h in (0, 1):
+        ring_in_stage[h, 0] = both_in(h, 0).astype(jnp.bfloat16)
+        ring_copy(h, 0, 0).start()
+        ring_out_stage[h, 0] = both_out(h, 0).astype(jnp.bfloat16)
+        ring_copy(h, 0, 1).start()
+        ring_out_stage[h, 2] = both_out(h, 1).astype(jnp.bfloat16)
+        ring_copy(h, 2, 1).start()
+        ring_in_stage[h, 2] = both_in(h, 2).astype(jnp.bfloat16)
+        ring_copy(h, 2, 0).start()
+        sum_in[h] = both_in(h, 3)
+        sum_out[h] = both_out(h, 3)
+    for h in (0, 1):
+        own = both_in(h, 1)
+        ring_copy(h, 0, 0).wait_recv()
+        ring_in_stage[h, 1] = (own + ring_in[h, 0].astype(jnp.float32)).astype(jnp.bfloat16)
+        ring_copy(h, 1, 0).start()
+        own = both_out(h, 2)
+        ring_copy(h, 0, 1).wait_recv()
+        ring_out_stage[h, 1] = (own + ring_out[h, 0].astype(jnp.float32)).astype(jnp.bfloat16)
+        ring_copy(h, 1, 1).start()
+
+    def total(h, piece):
+        kept, land = ((sum_in, ring_in), (sum_out, ring_out))[piece]
+        for slot in (2, 1):
+            ring_copy(h, slot, piece).wait_recv()
+        return kept[h] + land[h, 1].astype(jnp.float32) + land[h, 2].astype(jnp.float32)
+
+    far_in_stage[...] = total(0, 0).astype(jnp.bfloat16)
+    far_copy(0).start()
+    far_out_stage[...] = total(0, 1).astype(jnp.bfloat16)
+    far_copy(1).start()
+    own = total(1, 0)
+    far_copy(0).wait_recv()
+    gin_ref[...] = ((own + far_in[...].astype(jnp.float32)) * gain_ref[...]).astype(jnp.bfloat16)
+    own = total(1, 1)
+    far_copy(1).wait_recv()
+    gout_ref[...] = (own + far_out[...].astype(jnp.float32)).astype(jnp.bfloat16)
+
+    for j, piece, way in sent:
+        spread(j, piece, way).wait_send()
+    for piece in (0, 1):
+        far_copy(piece).wait_send()
+        for m in range(8):
+            pair_copy(m, piece).wait_send()
+        for h in (0, 1):
+            for slot in range(3):
+                ring_copy(h, slot, piece).wait_send()
 
     @pl.when(s < stages - 1)
     def _():
@@ -176,39 +336,45 @@
     inner = proj_in.shape[2]
     share = features // shards
     gain = lax.dynamic_slice_in_dim(norm_gain[0], f * share, share)[:, None]
-    scaled_in = (proj_in[0].astype(jnp.float32) * gain).astype(jnp.bfloat16)
-    weight_in = lax.all_gather(scaled_in, "fsdp", axis=0, tiled=True)
-    weight_out = lax.all_gather(proj_out[0], "fsdp", axis=1, tiled=True)
     blocks = latents.shape[0] * latents.shape[1] // ROWS
     lat = latents.reshape(blocks, ROWS, features)
     up = upstream.reshape(blocks, ROWS, features)
     vmem = pl.BlockSpec(memory_space=pltpu.VMEM)
     anywhere = pl.BlockSpec(memory_space=pl.ANY)
-    wide_buffer = pltpu.VMEM((blocks, ROWS, features), jnp.bfloat16)
-    narrow = pltpu.VMEM((blocks, ROWS, inner), jnp.bfloat16)
-    narrow_f32 = pltpu.VMEM((blocks, ROWS, inner), jnp.float32)
-    sems = pltpu.SemaphoreType.DMA((blocks, CHUNKS))
-    part_in, part_out = pl.pallas_call(
+
+    def low(*shape):
+        return pltpu.VMEM(shape, jnp.bfloat16)
+
+    def high(*shape):
+        return pltpu.VMEM(shape, jnp.float32)
+
+    def sems(*shape):
+        return pltpu.SemaphoreType.DMA(shape)
+
+    tall, flat = (share, inner), (inner, share)
+    grad_in, grad_out = pl.pallas_call(
         functools.partial(relay_kernel, stages, blocks, features),
         out_shape=(
-            jax.ShapeDtypeStruct((features, inner), jnp.bfloat16),
-            jax.ShapeDtypeStruct((inner, features), jnp.bfloat16),
+            jax.ShapeDtypeStruct(tall, jnp.bfloat16),
+            jax.ShapeDtypeStruct(flat, jnp.bfloat16),
         ),
-        in_specs=[anywhere, anywhere, vmem, vmem],
+        in_specs=[anywhere, anywhere, vmem, vmem, vmem],
         out_specs=(vmem, vmem),
         scratch_shapes=[
-            wide_buffer, wide_buffer, wide_buffer, wide_buffer,
-            narrow, narrow_f32, narrow_f32, narrow_f32, narrow,
-            sems, sems, sems, sems,
+            low(features, inner), low(inner, features),
+            *[low(blocks, ROWS, features)] * 4,
+            low(blocks, ROWS, inner), *[high(blocks, ROWS, inner)] * 3, low(blocks, ROWS, inner),
+            low(8, *tall), low(8, *flat), low(8, *tall), low(8, *flat),
+            low(2, 3, *tall), low(2, 3, *flat), low(2, 3, *tall), low(2, 3, *flat),
+            low(*tall), low(*flat), low(*tall), low(*flat), high(2, *tall), high(2, *flat),
+            *[sems(blocks, CHUNKS)] * 4, sems(4, shards, 2), sems(shards, 2),
+            sems(8, 2), sems(8, 2), sems(2, 3, 2), sems(2, 3, 2), sems(2), sems(2),
         ],
         compiler_params=pltpu.CompilerParams(
             collective_id=0, has_side_effects=True, vmem_limit_bytes=48 * 1024 * 1024
         ),
         name="relay",
-    )(lat, up, weight_in, weight_out)
-    grad_in = lax.psum_scatter(part_in, "fsdp", scatter_dimension=0, tiled=True)
-    grad_out = lax.psum_scatter(part_out, "fsdp", scatter_dimension=1, tiled=True)
-    grad_in = (grad_in.astype(jnp.float32) * gain).astype(jnp.bfloat16)
+    )(lat, up, proj_in[0], proj_out[0], gain)
     return grad_in[None], grad_out[None]
 
 

time: 614 us -> 337 us (0.55)
  waiting for transfers between devices: 327 us -> 0 us
  Pallas kernels: 260 us -> 329 us
  between operations: 13.8 us -> 0.67 us
    all_gather x2 -> x0, waiting for transfers between devices: 144 us -> none  [the longest x1 74.1 us: per_device(): weight_out = lax.all_gather(proj_out[0], 'fsdp', axis=1, tiled=True)]
    reduce_scatter x1 -> x0, waiting for transfers between devices: 94 us -> none  [per_device(): grad_in = lax.psum_scatter(part_in, 'fsdp', scatter_dimension=0, tiled=True)]
    unnamed x5 -> x0, waiting for transfers between devices: 89 us -> none
    pallas_call x1, Pallas kernels: 260 us -> 329 us  [per_device(): pl.pallas_call(functools.partial(relay_kernel, stages, blocks, features),...]
  transfers between devices with their start and end apart: 4 -> 0, of which waited for: 4 -> 0; matrix products, arithmetic and copies ran while one was open for 1% -> 0% of each run, Pallas kernels for 0% -> 0%
where the time goes in v2:
time: 337 us; the launch traced here: 336 us
  Pallas kernels  329 us (98%)
  local copies, waits for them, and re-layouts  6.89 us (2%)
    pallas_call x1, Pallas kernels, per_device(): pl.pallas_call(functools.partial(relay_kernel, stages, blocks, features),...  329 us
    unnamed x12, local copies, waits for them, and re-layouts  6.75 us

profile of v2, /device:TPU:2, one launch (start us, length us, event | category | flops | bytes accessed | tf_op | source)
XLA Modules:
  0.0 336.4 jit_solution(17350152064880535692)
XLA Ops:
  0.6 0.0 copy-start
  0.6 0.7 copy-done
  1.4 0.1 copy.7.gain_ref
  1.5 0.0 copy-start.1
  1.5 1.4 copy-done.1
  2.9 0.0 copy-start.2
  2.9 1.4 copy-done.2
  4.3 0.0 copy-start.3
  4.3 0.9 copy-done.3
  5.3 0.0 copy-start.4
  5.3 0.9 copy-done.4
  6.2 328.9 %relay.1 = (bf16[384,256]{1,0:T(8,128)(2,1)S(1)}, bf16[256,384]{1,0:T(8,128)(2,1)S(1)}) custom-call(bf16[8,16,6144]{2,1,0:T(8,128)(2,1)S(1)} %bitcast.8, bf16[8,16,6144]{2,1,0:T(8,128)(2,1)S(1)} %bitcast.9, bf16[384,256]{1,0:T(8,128)(2,1)S(1)} %bitcast.10, bf16[256,384]{1,0:T(8,128)(2,1)S(1)} %bitcast.11, f32[384,1]{1,0:T(8,128)S(1)} %copy.7.gain_ref), custom_call_target="tpu_custom_call" | custom-call | tf_op jit(solution)/shard_map/relay/pallas_call | solution.py:355
  335.1 0.7 copy.10
  335.7 0.7 copy.11
  (1 shorter events, 0.0 us)
Async XLA Ops:
  0.6 0.7 copy-start
  1.5 1.4 copy-start.1
  2.9 1.4 copy-start.2
  4.3 0.9 copy-start.3
  5.3 0.9 copy-start.4

commit v3 on v2

--- a/solution.py
+++ b/solution.py
@@ -11,24 +11,28 @@
 epsilon = 1e-06
 root_half = 0.7071067811865476
 inv_root_tau = 0.3989422804014327
+TOKENS = 8
 ROWS = 16
 CHUNKS = 3
+LAG = 2
 
 
 def relay_kernel(
     stages, blocks, features,
     lat_ref, up_ref, pin_ref, pout_ref, gain_ref, gin_ref, gout_ref,
-    win_ref, wout_ref,
-    h_in, h_out, g_in, g_out, act_s, slope_s, pre_s, inv_s, q_s,
+    win_ref, wout_ref, win_t, wout_t, own_in, own_gain, gain_s, top,
+    h_in, h_out, g_in, g_out, slope_s, pre_s, inv_s, act_s, q_s,
     pair_in, pair_out, pair_in_stage, pair_out_stage,
     ring_in, ring_out, ring_in_stage, ring_out_stage,
     far_in, far_out, far_in_stage, far_out_stage, sum_in, sum_out,
-    f_send, f_recv, b_send, b_recv, ag_send, ag_recv,
+    load_sem, top_sem, f_send, f_recv, b_send, b_recv, ag_send, ag_recv,
     pair_send, pair_recv, ring_send, ring_recv, far_send, far_recv,
 ):
     s = lax.axis_index("pipe")
     f = lax.axis_index("fsdp")
-    wide = features // CHUNKS
+    fold = features // 2
+    wide = fold // CHUNKS
+    inner = pin_ref.shape[1]
     share = pin_ref.shape[0]
     after = lax.rem(s + 1, stages)
     before = lax.rem(s + stages - 1, stages)
@@ -44,15 +48,29 @@
     pair = index_of(half, place, 1 - core)
     far = index_of(1 - half, place, core)
 
+    def rows_of(j):
+        return pl.ds(pl.multiple_of(j * share, 128), share)
+
+    loads = (
+        pltpu.make_async_copy(gain_ref.at[:, rows_of(f)], own_gain, load_sem.at[0]),
+        pltpu.make_async_copy(pin_ref, own_in, load_sem.at[1]),
+        pltpu.make_async_copy(pout_ref, wout_ref.at[:, rows_of(f)], load_sem.at[2]),
+    )
+    for load in loads:
+        load.start()
+
     barrier = pltpu.get_barrier_semaphore()
     for other in ((before, f), (after, f), (s, right), (s, left), (s, pair), (s, far)):
         pl.semaphore_signal(barrier, inc=1, device_id=other, device_id_type=MESH)
 
-    def rows_of(j):
-        return pl.ds(pl.multiple_of(j * share, 128), share)
-
-    win_ref[rows_of(f), :] = (pin_ref[...].astype(jnp.float32) * gain_ref[...]).astype(jnp.bfloat16)
-    wout_ref[:, rows_of(f)] = pout_ref[...]
+    for load in loads:
+        load.wait()
+    gain_s[...] = jnp.broadcast_to(own_gain[...], (128, share)).T
+
+    def gains():
+        return jnp.concatenate([gain_s[...]] * (inner // 128), axis=1)
+
+    win_ref[rows_of(f), :] = (own_in[...].astype(jnp.float32) * gains()).astype(jnp.bfloat16)
     pl.semaphore_wait(barrier, 6)
 
     routes = (far, right, left, pair)
@@ -77,8 +95,15 @@
     def arrived(j, piece):
         spread(j, piece, 3).wait_recv()
 
+    def reach_far(turn):
+        @pl.when(lax.rem(s, 4) == turn)
+        def _():
+            for piece in (0, 1):
+                spread(f, piece, 0).start()
+
     for piece in (0, 1):
-        share_out(f, piece, 0)
+        sent.append((f, piece, 0))
+    reach_far(0)
     for piece in (0, 1):
         share_out(f, piece, 1, 2)
     for piece in (0, 1):
@@ -101,23 +126,34 @@
             device_id=(before, f), device_id_type=MESH,
         )
 
+    def folded(upper, lower):
+        return jnp.concatenate([upper, lower], axis=0)
+
+    def load_folded(source, target, land, sem):
+        load = pltpu.make_async_copy(source, top, top_sem)
+        load.start()
+        load.wait()
+
+        @pl.loop(0, blocks // 2)
+        def _(i):
+            for c in range(CHUNKS):
+                low = top[i, :, columns(c)].astype(jnp.float32)
+                high = top[i, :, pl.ds(fold + c * wide, wide)].astype(jnp.float32)
+                for k in (0, 1):
+                    rows = slice(k * TOKENS, (k + 1) * TOKENS)
+                    target[2 * i + k, :, columns(c)] = folded(low[rows], high[rows]).astype(jnp.bfloat16)
+                    pltpu.make_async_copy(
+                        target.at[2 * i + k, :, columns(c)], land.at[2 * i + k, :, columns(c)],
+                        sem.at[2 * i + k, c],
+                    ).start()
+
     @pl.when(s == 0)
     def _():
-        @pl.loop(0, blocks)
-        def _(i):
-            for c in range(CHUNKS):
-                pltpu.make_async_copy(
-                    lat_ref.at[i, :, columns(c)], h_in.at[i, :, columns(c)], f_recv.at[i, c]
-                ).start()
+        load_folded(lat_ref, g_out, h_in, f_recv)
 
     @pl.when(s == stages - 1)
     def _():
-        @pl.loop(0, blocks)
-        def _(i):
-            for c in range(CHUNKS):
-                pltpu.make_async_copy(
-                    up_ref.at[i, :, columns(c)], g_in.at[i, :, columns(c)], b_recv.at[i, c]
-                ).start()
+        load_folded(up_ref, h_out, g_in, b_recv)
 
     for z in (half, 1 - half):
         mine, on_left, on_right, across = [index_of(z, place + step, core) for step in (0, -1, 1, 2)]
@@ -127,79 +163,122 @@
                 share_out(mine, piece, 1, 2, 3)
         arrived(on_left, 0)
         share_out(on_left, 0, 1, 3)
+        if z is half:
+            reach_far(1)
         arrived(on_right, 0)
         share_out(on_right, 0, 3)
         arrived(on_right, 1)
         share_out(on_right, 1, 2, 3)
         arrived(on_left, 1)
         share_out(on_left, 1, 3)
+        if z is half:
+            reach_far(2)
         for piece in (0, 1):
             arrived(across, piece)
             share_out(across, piece, 3)
+        if z is half:
+            reach_far(3)
     for z in (half, 1 - half):
         for step in (0, -1, 1, 2):
             for piece in (0, 1):
                 arrived(index_of(z, place + step, 1 - core), piece)
+    def transpose_weights():
+        @pl.loop(0, features // 512)
+        def _(n):
+            cut = pl.ds(pl.multiple_of(n * 512, 512), 512)
+            wout_t[cut, :] = wout_ref[:, cut].T
+            win_t[:, cut] = win_ref[cut, :].T
+
     def forward(i):
-        pre = jnp.zeros((ROWS, win_ref.shape[1]), jnp.float32)
+        low = jnp.zeros((ROWS, inner), jnp.float32)
+        high = jnp.zeros((ROWS, inner), jnp.float32)
         square = jnp.zeros((ROWS, 1), jnp.float32)
         for c in range(CHUNKS):
             f_copy(i, c).wait_recv()
             h = h_in[i, :, columns(c)]
-            pre += jnp.dot(h, win_ref[columns(c), :], preferred_element_type=jnp.float32)
+            low += jnp.dot(h, win_ref[columns(c), :], preferred_element_type=jnp.float32)
+            high += jnp.dot(
+                h, win_ref[pl.ds(fold + c * wide, wide), :], preferred_element_type=jnp.float32
+            )
             wide_h = h.astype(jnp.float32)
             square += jnp.sum(wide_h * wide_h, axis=-1, keepdims=True)
+        square = square[:TOKENS] + square[TOKENS:]
         inverse = lax.rsqrt(square * (1.0 / features) + epsilon)
-        pre = pre * inverse
+        pre = (low[:TOKENS] + high[TOKENS:]) * inverse
         cdf = 0.5 * (1.0 + lax.erf(pre * root_half))
-        act = (pre * cdf).astype(jnp.bfloat16)
+        act = pre * cdf
 
         @pl.when(s < stages - 1)
         def _():
+            both = folded(act, act).astype(jnp.bfloat16)
             for c in range(CHUNKS):
-                branch = jnp.dot(act, wout_ref[:, columns(c)], preferred_element_type=jnp.float32)
+                upper = jnp.dot(both, wout_ref[:, columns(c)], preferred_element_type=jnp.float32)
+                lower = jnp.dot(
+                    both, wout_ref[:, pl.ds(fold + c * wide, wide)],
+                    preferred_element_type=jnp.float32,
+                )
                 h_out[i, :, columns(c)] = (
-                    h_in[i, :, columns(c)].astype(jnp.float32) + branch
+                    h_in[i, :, columns(c)].astype(jnp.float32)
+                    + folded(upper[:TOKENS], lower[TOKENS:])
                 ).astype(jnp.bfloat16)
                 f_copy(i, c).start()
 
-        act_s[i] = act
+        blank = jnp.zeros_like(act)
+        act_s[0, i] = folded(act, blank).astype(jnp.bfloat16)
+        act_s[1, i] = folded(blank, act).astype(jnp.bfloat16)
         pre_s[i] = pre
         slope_s[i] = cdf + pre * jnp.exp(-0.5 * pre * pre) * inv_root_tau
         inv_s[i] = jnp.broadcast_to(inverse, pre.shape)
 
     def backward(i):
-        grad_act = jnp.zeros((ROWS, win_ref.shape[1]), jnp.float32)
+        low = jnp.zeros((ROWS, inner), jnp.float32)
+        high = jnp.zeros((ROWS, inner), jnp.float32)
         for c in range(CHUNKS):
             b_copy(i, c).wait_recv()
-            grad_act += lax.dot_general(
-                g_in[i, :, columns(c)], wout_ref[:, columns(c)], (((1,), (1,)), ((), ())),
-                preferred_element_type=jnp.float32,
+            g = g_in[i, :, columns(c)]
+            low += jnp.dot(g, wout_t[columns(c), :], preferred_element_type=jnp.float32)
+            high += jnp.dot(
+                g, wout_t[pl.ds(fold + c * wide, wide), :], preferred_element_type=jnp.float32
             )
-        grad_pre = grad_act * slope_s[i]
+        grad_pre = (low[:TOKENS] + high[TOKENS:]) * slope_s[i]
         inverse = inv_s[i]
         mean = jnp.sum(grad_pre * pre_s[i], axis=-1, keepdims=True) * (1.0 / features)
-        q = (grad_pre * inverse).astype(jnp.bfloat16)
-        q_s[i] = q
+        q = grad_pre * inverse
         pull = inverse[:, :1] * inverse[:, :1] * mean
 
         @pl.when(s > 0)
         def _():
+            both = folded(q, q).astype(jnp.bfloat16)
+            pulls = folded(pull, pull)
             for c in range(CHUNKS):
-                path = lax.dot_general(
-                    q, win_ref[columns(c), :], (((1,), (1,)), ((), ())),
+                upper = jnp.dot(both, win_t[:, columns(c)], preferred_element_type=jnp.float32)
+                lower = jnp.dot(
+                    both, win_t[:, pl.ds(fold + c * wide, wide)],
                     preferred_element_type=jnp.float32,
                 )
                 g_out[i, :, columns(c)] = (
-                    g_in[i, :, columns(c)].astype(jnp.float32) + path
-                    - pull * h_in[i, :, columns(c)].astype(jnp.float32)
+                    g_in[i, :, columns(c)].astype(jnp.float32)
+                    + folded(upper[:TOKENS], lower[TOKENS:])
+                    - pulls * h_in[i, :, columns(c)].astype(jnp.float32)
                 ).astype(jnp.bfloat16)
                 b_copy(i, c).start()
 
-    @pl.loop(0, blocks + 2 * stages - 2)
+        blank = jnp.zeros_like(q)
+        q_s[0, i] = folded(q, blank).astype(jnp.bfloat16)
+        q_s[1, i] = folded(blank, q).astype(jnp.bfloat16)
+
+    @pl.when(s >= 4)
+    def _():
+        transpose_weights()
+
+    @pl.loop(0, blocks + LAG * (2 * stages - 2))
     def _(tick):
-        ahead = tick - s
-        back = tick - (2 * stages - 2) + s
+        @pl.when((s < 4) & (tick == LAG * s + blocks))
+        def _():
+            transpose_weights()
+
+        ahead = tick - LAG * s
+        back = tick - LAG * (2 * stages - 2 - s)
 
         @pl.when((ahead >= 0) & (ahead < blocks))
         def _():
@@ -209,18 +288,21 @@
         def _():
             backward(back)
 
-    tokens = blocks * ROWS
-    q_all = q_s[...].reshape(tokens, -1)
-    act_all = act_s[...].reshape(tokens, -1)
-    over_tokens = (((0,), (0,)), ((), ()))
+    rows = blocks * ROWS
+    over_rows = (((0,), (0,)), ((), ()))
+
+    def cut_of(j):
+        return pl.ds(pl.multiple_of(lax.rem(j, 8) * share, 128), share)
 
     def part_in(j):
-        h = h_in[:, :, rows_of(j)].reshape(tokens, share)
-        return lax.dot_general(h, q_all, over_tokens, preferred_element_type=jnp.float32)
+        h = h_in[:, :, cut_of(j)].reshape(rows, share)
+        q = q_s[j // 8].reshape(rows, inner)
+        return lax.dot_general(h, q, over_rows, preferred_element_type=jnp.float32)
 
     def part_out(j):
-        g = g_in[:, :, rows_of(j)].reshape(tokens, share)
-        return lax.dot_general(act_all, g, over_tokens, preferred_element_type=jnp.float32)
+        g = g_in[:, :, cut_of(j)].reshape(rows, share)
+        act = act_s[j // 8].reshape(rows, inner)
+        return lax.dot_general(act, g, over_rows, preferred_element_type=jnp.float32)
 
     def remote(src, dst, send, recv, route):
         return pltpu.make_async_remote_copy(
@@ -246,7 +328,7 @@
 
     steps = (2, 1, -1, 0)
     halves = (1 - half, half)
-    for h in (0, 1):
+    def pair_share(h):
         for k, step in enumerate(steps):
             m = h * 4 + k
             j = index_of(halves[h], place + step, 1 - core)
@@ -265,7 +347,7 @@
         j = index_of(halves[h], place + steps[k], core)
         return part_out(j) + pair_out[h * 4 + k].astype(jnp.float32)
 
-    for h in (0, 1):
+    def open_ring(h):
         ring_in_stage[h, 0] = both_in(h, 0).astype(jnp.bfloat16)
         ring_copy(h, 0, 0).start()
         ring_out_stage[h, 0] = both_out(h, 0).astype(jnp.bfloat16)
@@ -276,7 +358,8 @@
         ring_copy(h, 2, 0).start()
         sum_in[h] = both_in(h, 3)
         sum_out[h] = both_out(h, 3)
-    for h in (0, 1):
+
+    def relay_ring(h):
         own = both_in(h, 1)
         ring_copy(h, 0, 0).wait_recv()
         ring_in_stage[h, 1] = (own + ring_in[h, 0].astype(jnp.float32)).astype(jnp.bfloat16)
@@ -292,13 +375,19 @@
             ring_copy(h, slot, piece).wait_recv()
         return kept[h] + land[h, 1].astype(jnp.float32) + land[h, 2].astype(jnp.float32)
 
+    pair_share(0)
+    open_ring(0)
+    pair_share(1)
+    relay_ring(0)
+    open_ring(1)
     far_in_stage[...] = total(0, 0).astype(jnp.bfloat16)
     far_copy(0).start()
     far_out_stage[...] = total(0, 1).astype(jnp.bfloat16)
     far_copy(1).start()
+    relay_ring(1)
     own = total(1, 0)
     far_copy(0).wait_recv()
-    gin_ref[...] = ((own + far_in[...].astype(jnp.float32)) * gain_ref[...]).astype(jnp.bfloat16)
+    gin_ref[...] = ((own + far_in[...].astype(jnp.float32)) * gains()).astype(jnp.bfloat16)
     own = total(1, 1)
     far_copy(1).wait_recv()
     gout_ref[...] = (own + far_out[...].astype(jnp.float32)).astype(jnp.bfloat16)
@@ -331,16 +420,14 @@
 def per_device(latents, upstream, proj_in, proj_out, norm_gain):
     stages = lax.axis_size("pipe")
     shards = lax.axis_size("fsdp")
-    f = lax.axis_index("fsdp")
     features = latents.shape[2]
     inner = proj_in.shape[2]
     share = features // shards
-    gain = lax.dynamic_slice_in_dim(norm_gain[0], f * share, share)[:, None]
-    blocks = latents.shape[0] * latents.shape[1] // ROWS
-    lat = latents.reshape(blocks, ROWS, features)
-    up = upstream.reshape(blocks, ROWS, features)
+    blocks = latents.shape[0] * latents.shape[1] // TOKENS
+    lat = latents.reshape(blocks // 2, ROWS, features)
+    up = upstream.reshape(blocks // 2, ROWS, features)
     vmem = pl.BlockSpec(memory_space=pltpu.VMEM)
-    anywhere = pl.BlockSpec(memory_space=pl.ANY)
+    anywhere = pl.BlockSpec(memory_space=pltpu.HBM)
 
     def low(*shape):
         return pltpu.VMEM(shape, jnp.bfloat16)
@@ -358,23 +445,24 @@
             jax.ShapeDtypeStruct(tall, jnp.bfloat16),
             jax.ShapeDtypeStruct(flat, jnp.bfloat16),
         ),
-        in_specs=[anywhere, anywhere, vmem, vmem, vmem],
+        in_specs=[anywhere] * 5,
         out_specs=(vmem, vmem),
         scratch_shapes=[
-            low(features, inner), low(inner, features),
-            *[low(blocks, ROWS, features)] * 4,
-            low(blocks, ROWS, inner), *[high(blocks, ROWS, inner)] * 3, low(blocks, ROWS, inner),
+            low(features, inner), low(inner, features), low(inner, features), low(features, inner),
+            low(*tall), high(1, share), high(share, 128),
+            low(blocks // 2, ROWS, features), *[low(blocks, ROWS, features // 2)] * 4,
+            *[high(blocks, TOKENS, inner)] * 3, *[low(2, blocks, ROWS, inner)] * 2,
             low(8, *tall), low(8, *flat), low(8, *tall), low(8, *flat),
             low(2, 3, *tall), low(2, 3, *flat), low(2, 3, *tall), low(2, 3, *flat),
             low(*tall), low(*flat), low(*tall), low(*flat), high(2, *tall), high(2, *flat),
-            *[sems(blocks, CHUNKS)] * 4, sems(4, shards, 2), sems(shards, 2),
+            sems(3), pltpu.SemaphoreType.DMA, *[sems(blocks, CHUNKS)] * 4, sems(4, shards, 2), sems(shards, 2),
             sems(8, 2), sems(8, 2), sems(2, 3, 2), sems(2, 3, 2), sems(2), sems(2),
         ],
         compiler_params=pltpu.CompilerParams(
             collective_id=0, has_side_effects=True, vmem_limit_bytes=48 * 1024 * 1024
         ),
         name="relay",
-    )(lat, up, proj_in[0], proj_out[0], gain)
+    )(lat, up, proj_in[0], proj_out[0], norm_gain)
     return grad_in[None], grad_out[None]
 
 

time: 337 us -> 275 us (0.82)
  Pallas kernels: 329 us -> 267 us
    pallas_call x1, Pallas kernels: 329 us -> 267 us  [per_device(): pl.pallas_call(functools.partial(relay_kernel, stages, blocks, features),...]
where the time goes in v3:
time: 275 us
  Pallas kernels  267 us (97%)
  local copies, waits for them, and re-layouts  6.75 us (2%)
    pallas_call x1, Pallas kernels, per_device(): pl.pallas_call(functools.partial(relay_kernel, stages, blocks, features),...  267 us
    unnamed x12, local copies, waits for them, and re-layouts  6.75 us

profile of v3, /device:TPU:2, one launch (start us, length us, event | category | flops | bytes accessed | tf_op | source)
XLA Modules:
  0.0 274.6 jit_solution(3654484519913222964)
XLA Ops:
  0.6 0.0 copy-start
  0.6 1.4 copy-done
  2.0 0.0 copy-start.1
  2.0 1.4 copy-done.1
  3.4 0.0 copy-start.2
  3.5 0.9 copy-done.2
  4.4 0.0 copy-start.3
  4.4 0.9 copy-done.3
  5.3 0.0 copy-start.4
  5.3 0.7 copy-done.4
  6.0 267.2 %relay.1 = (bf16[384,256]{1,0:T(8,128)(2,1)S(1)}, bf16[256,384]{1,0:T(8,128)(2,1)S(1)}) custom-call(bf16[8,16,6144]{2,1,0:T(8,128)(2,1)S(1)} %bitcast.6, bf16[8,16,6144]{2,1,0:T(8,128)(2,1)S(1)} %bitcast.7, bf16[384,256]{1,0:T(8,128)(2,1)S(1)} %bitcast.8, bf16[256,384]{1,0:T(8,128)(2,1)S(1)} %bitcast.9, f32[1,6144]{1,0:T(1,128)S(1)} %copy-done.4), custom_call_target="tpu_custom_call" | custom-call | tf_op jit(solution)/shard_map/relay/pallas_call | solution.py:442
  273.3 0.7 copy.9
  273.9 0.7 copy.10
Async XLA Ops:
  0.6 1.4 copy-start
  2.0 1.4 copy-start.1
  3.4 0.9 copy-start.2
  4.4 0.9 copy-start.3
  5.3 0.7 copy-start.4

commit v4 on v3

--- a/solution.py
+++ b/solution.py
@@ -15,6 +15,7 @@
 ROWS = 16
 CHUNKS = 3
 LAG = 2
+VMEM_BYTES = 64 * 1024 * 1024 - 65536
 
 
 def relay_kernel(
@@ -26,7 +27,7 @@
     ring_in, ring_out, ring_in_stage, ring_out_stage,
     far_in, far_out, far_in_stage, far_out_stage, sum_in, sum_out,
     load_sem, top_sem, f_send, f_recv, b_send, b_recv, ag_send, ag_recv,
-    pair_send, pair_recv, ring_send, ring_recv, far_send, far_recv,
+    pair_send, pair_recv, ring_send, ring_recv, far_send, far_recv, turn,
 ):
     s = lax.axis_index("pipe")
     f = lax.axis_index("fsdp")
@@ -71,60 +72,8 @@
         return jnp.concatenate([gain_s[...]] * (inner // 128), axis=1)
 
     win_ref[rows_of(f), :] = (own_in[...].astype(jnp.float32) * gains()).astype(jnp.bfloat16)
-    pl.semaphore_wait(barrier, 6)
-
-    routes = (far, right, left, pair)
-
-    def shard(j, piece):
-        return win_ref.at[rows_of(j), :] if piece == 0 else wout_ref.at[:, rows_of(j)]
-
-    def spread(j, piece, route):
-        return pltpu.make_async_remote_copy(
-            src_ref=shard(j, piece), dst_ref=shard(j, piece),
-            send_sem=ag_send.at[route, j, piece], recv_sem=ag_recv.at[j, piece],
-            device_id=(s, routes[route]), device_id_type=MESH,
-        )
-
-    sent = []
-
-    def share_out(j, piece, *ways):
-        for way in ways:
-            spread(j, piece, way).start()
-            sent.append((j, piece, way))
-
-    def arrived(j, piece):
-        spread(j, piece, 3).wait_recv()
-
-    def reach_far(turn):
-        @pl.when(lax.rem(s, 4) == turn)
-        def _():
-            for piece in (0, 1):
-                spread(f, piece, 0).start()
-
-    for piece in (0, 1):
-        sent.append((f, piece, 0))
-    reach_far(0)
-    for piece in (0, 1):
-        share_out(f, piece, 1, 2)
-    for piece in (0, 1):
-        share_out(f, piece, 3)
-
     def columns(c):
         return pl.ds(c * wide, wide)
-
-    def f_copy(i, c):
-        return pltpu.make_async_remote_copy(
-            src_ref=h_out.at[i, :, columns(c)], dst_ref=h_in.at[i, :, columns(c)],
-            send_sem=f_send.at[i, c], recv_sem=f_recv.at[i, c],
-            device_id=(after, f), device_id_type=MESH,
-        )
-
-    def b_copy(i, c):
-        return pltpu.make_async_remote_copy(
-            src_ref=g_out.at[i, :, columns(c)], dst_ref=g_in.at[i, :, columns(c)],
-            send_sem=b_send.at[i, c], recv_sem=b_recv.at[i, c],
-            device_id=(before, f), device_id_type=MESH,
-        )
 
     def folded(upper, lower):
         return jnp.concatenate([upper, lower], axis=0)
@@ -154,6 +103,58 @@
     @pl.when(s == stages - 1)
     def _():
         load_folded(up_ref, h_out, g_in, b_recv)
+
+    pl.semaphore_wait(barrier, 6)
+
+    routes = (far, right, left, pair)
+
+    def shard(j, piece):
+        return win_ref.at[rows_of(j), :] if piece == 0 else wout_ref.at[:, rows_of(j)]
+
+    def spread(j, piece, route):
+        return pltpu.make_async_remote_copy(
+            src_ref=shard(j, piece), dst_ref=shard(j, piece),
+            send_sem=ag_send.at[route, j, piece], recv_sem=ag_recv.at[j, piece],
+            device_id=(s, routes[route]), device_id_type=MESH,
+        )
+
+    sent = []
+
+    def share_out(j, piece, *ways):
+        for way in ways:
+            spread(j, piece, way).start()
+            sent.append((j, piece, way))
+
+    def arrived(j, piece):
+        spread(j, piece, 3).wait_recv()
+
+    def reach_far(turn):
+        @pl.when(lax.rem(s, 4) == turn)
+        def _():
+            for piece in (0, 1):
+                spread(f, piece, 0).start()
+
+    for piece in (0, 1):
+        sent.append((f, piece, 0))
+    reach_far(0)
+    for piece in (0, 1):
+        share_out(f, piece, 1, 2)
+    for piece in (0, 1):
+        share_out(f, piece, 3)
+
+    def f_copy(i, c):
+        return pltpu.make_async_remote_copy(
+            src_ref=h_out.at[i, :, columns(c)], dst_ref=h_in.at[i, :, columns(c)],
+            send_sem=f_send.at[i, c], recv_sem=f_recv.at[i, c],
+            device_id=(after, f), device_id_type=MESH,
+        )
+
+    def b_copy(i, c):
+        return pltpu.make_async_remote_copy(
+            src_ref=g_out.at[i, :, columns(c)], dst_ref=g_in.at[i, :, columns(c)],
+            send_sem=b_send.at[i, c], recv_sem=b_recv.at[i, c],
+            device_id=(before, f), device_id_type=MESH,
+        )
 
     for z in (half, 1 - half):
         mine, on_left, on_right, across = [index_of(z, place + step, core) for step in (0, -1, 1, 2)]
@@ -282,7 +283,15 @@
 
         @pl.when((ahead >= 0) & (ahead < blocks))
         def _():
+            @pl.when((s == 0) & (core == 1) & (ahead == 0))
+            def _():
+                pl.semaphore_wait(turn, 1)
+
             forward(ahead)
+
+            @pl.when((s == 0) & (core == 0) & (ahead == 0))
+            def _():
+                pl.semaphore_signal(turn, inc=1, device_id=(s, pair), device_id_type=MESH)
 
         @pl.when((back >= 0) & (back < blocks))
         def _():
@@ -457,9 +466,10 @@
             low(*tall), low(*flat), low(*tall), low(*flat), high(2, *tall), high(2, *flat),
             sems(3), pltpu.SemaphoreType.DMA, *[sems(blocks, CHUNKS)] * 4, sems(4, shards, 2), sems(shards, 2),
             sems(8, 2), sems(8, 2), sems(2, 3, 2), sems(2, 3, 2), sems(2), sems(2),
+            pltpu.SemaphoreType.REGULAR,
         ],
         compiler_params=pltpu.CompilerParams(
-            collective_id=0, has_side_effects=True, vmem_limit_bytes=48 * 1024 * 1024
+            collective_id=0, has_side_effects=True, vmem_limit_bytes=VMEM_BYTES
         ),
         name="relay",
     )(lat, up, proj_in[0], proj_out[0], norm_gain)

time: 275 us -> 271 us (0.985)
  local copies, waits for them, and re-layouts: 6.75 us -> 3.24 us
    unnamed x12 -> x2, local copies, waits for them, and re-layouts: 6.75 us -> 3.24 us
where the time goes in v4:
time: 271 us
  Pallas kernels  267 us (99%)
  local copies, waits for them, and re-layouts  3.24 us (1%)
    pallas_call x1, Pallas kernels, per_device(): pl.pallas_call(functools.partial(relay_kernel, stages, blocks, features),...  267 us

profile of v4, /device:TPU:2, one launch (start us, length us, event | category | flops | bytes accessed | tf_op | source)
XLA Modules:
  0.0 270.6 jit_solution(413590239606760699)
XLA Ops:
  0.6 266.7 %relay.1 = (bf16[384,256]{1,0:T(8,128)(2,1)}, bf16[256,384]{1,0:T(8,128)(2,1)}) custom-call(bf16[8,16,6144]{2,1,0:T(8,128)(2,1)} %bitcast.6, bf16[8,16,6144]{2,1,0:T(8,128)(2,1)} %bitcast.7, bf16[384,256]{1,0:T(8,128)(2,1)} %bitcast.8, bf16[256,384]{1,0:T(8,128)(2,1)} %bitcast.9, f32[1,6144]{1,0:T(1,128)} %gain_ref.1), custom_call_target="tpu_custom_call" | custom-call | tf_op jit(solution)/shard_map/relay/pallas_call | solution.py:451
  267.3 1.6 copy.9
  268.9 1.6 copy.10

commit v5 on v4

--- a/solution.py
+++ b/solution.py
@@ -337,10 +337,10 @@
 
     steps = (2, 1, -1, 0)
     halves = (1 - half, half)
-    def pair_share(h):
-        for k, step in enumerate(steps):
+    def pair_share(h, *turns):
+        for k in turns:
             m = h * 4 + k
-            j = index_of(halves[h], place + step, 1 - core)
+            j = index_of(halves[h], place + steps[k], 1 - core)
             pair_in_stage[m] = part_in(j).astype(jnp.bfloat16)
             pair_copy(m, 0).start()
             pair_out_stage[m] = part_out(j).astype(jnp.bfloat16)
@@ -356,11 +356,13 @@
         j = index_of(halves[h], place + steps[k], core)
         return part_out(j) + pair_out[h * 4 + k].astype(jnp.float32)
 
-    def open_ring(h):
+    def start_ring(h):
         ring_in_stage[h, 0] = both_in(h, 0).astype(jnp.bfloat16)
         ring_copy(h, 0, 0).start()
         ring_out_stage[h, 0] = both_out(h, 0).astype(jnp.bfloat16)
         ring_copy(h, 0, 1).start()
+
+    def open_ring(h):
         ring_out_stage[h, 2] = both_out(h, 1).astype(jnp.bfloat16)
         ring_copy(h, 2, 1).start()
         ring_in_stage[h, 2] = both_in(h, 2).astype(jnp.bfloat16)
@@ -384,10 +386,13 @@
             ring_copy(h, slot, piece).wait_recv()
         return kept[h] + land[h, 1].astype(jnp.float32) + land[h, 2].astype(jnp.float32)
 
-    pair_share(0)
+    pair_share(0, 0, 1)
+    start_ring(0)
+    pair_share(0, 2, 3)
     open_ring(0)
-    pair_share(1)
+    pair_share(1, 0, 1, 2, 3)
     relay_ring(0)
+    start_ring(1)
     open_ring(1)
     far_in_stage[...] = total(0, 0).astype(jnp.bfloat16)
     far_copy(0).start()

time: 271 us -> 273 us (level)
  no operation moved by 1% of the time
where the time goes in v5:
time: 273 us; the launch traced here: 271 us
  Pallas kernels  267 us (98%)
  local copies, waits for them, and re-layouts  3.24 us (1%)
    pallas_call x1, Pallas kernels, per_device(): pl.pallas_call(functools.partial(relay_kernel, stages, blocks, features),...  267 us

profile of v5, /device:TPU:2, one launch (start us, length us, event | category | flops | bytes accessed | tf_op | source)
XLA Modules:
  0.0 270.6 jit_solution(11639185709303756782)
XLA Ops:
  0.6 266.7 %relay.1 = (bf16[384,256]{1,0:T(8,128)(2,1)}, bf16[256,384]{1,0:T(8,128)(2,1)}) custom-call(bf16[8,16,6144]{2,1,0:T(8,128)(2,1)} %bitcast.6, bf16[8,16,6144]{2,1,0:T(8,128)(2,1)} %bitcast.7, bf16[384,256]{1,0:T(8,128)(2,1)} %bitcast.8, bf16[256,384]{1,0:T(8,128)(2,1)} %bitcast.9, f32[1,6144]{1,0:T(1,128)} %gain_ref.1), custom_call_target="tpu_custom_call" | custom-call | tf_op jit(solution)/shard_map/relay/pallas_call | solution.py:456
  267.3 1.6 copy.9
  268.9 1.6 copy.10

commit v6 on v4

--- a/solution.py
+++ b/solution.py
@@ -387,6 +387,23 @@
     pair_share(0)
     open_ring(0)
     pair_share(1)
+    for j, piece, way in sent:
+        spread(j, piece, way).wait_send()
+
+    @pl.when(s < stages - 1)
+    def _():
+        @pl.loop(0, blocks)
+        def _(i):
+            for c in range(CHUNKS):
+                f_copy(i, c).wait_send()
+
+    @pl.when(s > 0)
+    def _():
+        @pl.loop(0, blocks)
+        def _(i):
+            for c in range(CHUNKS):
+                b_copy(i, c).wait_send()
+
     relay_ring(0)
     open_ring(1)
     far_in_stage[...] = total(0, 0).astype(jnp.bfloat16)
@@ -401,8 +418,6 @@
     far_copy(1).wait_recv()
     gout_ref[...] = (own + far_out[...].astype(jnp.float32)).astype(jnp.bfloat16)
 
-    for j, piece, way in sent:
-        spread(j, piece, way).wait_send()
     for piece in (0, 1):
         far_copy(piece).wait_send()
         for m in range(8):
@@ -410,20 +425,6 @@
         for h in (0, 1):
             for slot in range(3):
                 ring_copy(h, slot, piece).wait_send()
-
-    @pl.when(s < stages - 1)
-    def _():
-        @pl.loop(0, blocks)
-        def _(i):
-            for c in range(CHUNKS):
-                f_copy(i, c).wait_send()
-
-    @pl.when(s > 0)
-    def _():
-        @pl.loop(0, blocks)
-        def _(i):
-            for c in range(CHUNKS):
-                b_copy(i, c).wait_send()
 
 
 def per_device(latents, upstream, proj_in, proj_out, norm_gain):

time: 271 us -> 271 us (level)
  no operation moved by 1% of the time
where the time goes in v6:
time: 271 us; the launch traced here: 270 us
  Pallas kernels  266 us (98%)
  local copies, waits for them, and re-layouts  3.24 us (1%)
    pallas_call x1, Pallas kernels, per_device(): pl.pallas_call(functools.partial(relay_kernel, stages, blocks, features),...  266 us

profile of v6, /device:TPU:2, one launch (start us, length us, event | category | flops | bytes accessed | tf_op | source)
XLA Modules:
  0.0 270.4 jit_solution(10733117270308343029)
XLA Ops:
  0.6 266.5 %relay.1 = (bf16[384,256]{1,0:T(8,128)(2,1)}, bf16[256,384]{1,0:T(8,128)(2,1)}) custom-call(bf16[8,16,6144]{2,1,0:T(8,128)(2,1)} %bitcast.6, bf16[8,16,6144]{2,1,0:T(8,128)(2,1)} %bitcast.7, bf16[384,256]{1,0:T(8,128)(2,1)} %bitcast.8, bf16[256,384]{1,0:T(8,128)(2,1)} %bitcast.9, f32[1,6144]{1,0:T(1,128)} %gain_ref.1), custom_call_target="tpu_custom_call" | custom-call | tf_op jit(solution)/shard_map/relay/pallas_call | solution.py:452
  267.1 1.6 copy.9
  268.7 1.6 copy.10
